TPU v7x, 32 devices: a whole 2x2x4 slice. The times are simulated.
32 devices in a mesh: req: 4 (over y, x), mlp: 8 (over z, core).
Axes of the slice: x: 2, y: 2, z: 4, core: 2. Of those that a mesh axis runs over, the one named last changes fastest.
Arguments:
- prompt_tokens: bfloat16 [8, 1024, 2048], P('req', None, 'mlp'), may hold values from -6 to 6
- decode_tokens: bfloat16 [16, 2048], P('req', 'mlp'), may hold values from -6 to 6
- prompt_lengths: int32 [8], P('req'), may hold values from 128 to 1024, as said below
- decode_states: float32 [16, 16, 128, 128], P('req', 'mlp'), may hold values from -6 to 6
- w_fio: float32 [2048, 6144], P('req', 'mlp'), may hold values from -0.125 to 0.125
- forget_bias: float32 [2048], P('mlp'), as said below
- head_gain: float32 [2048], P('mlp'), may hold values from 0.1 to 1.9
- w_out: float32 [2048, 2048], P('mlp', 'req'), may hold values from -0.125 to 0.125
- mlp_gain: float32 [2048], replicated, may hold values from 0.1 to 1.9
- w_gu: float32 [2048, 11264], P('req', 'mlp'), may hold values from -0.125 to 0.125
- w_down: float32 [5632, 2048], P('mlp', 'req'), may hold values from -0.078125 to 0.078125
Outputs:
- prompt_out: bfloat16 [8, 1024, 2048], P('req', None, 'mlp')
- decode_out: bfloat16 [16, 2048], P('req', 'mlp')
- prompt_states: float32 [8, 16, 128, 128], P('req', 'mlp')
- decode_next: float32 [16, 16, 128, 128], P('req', 'mlp')
Inputs may be any that keep to these rules, and one draw needn't show every extreme that they name: `prompt_lengths`: slots at or past a prompt's length are padding; one prompt has length 1024 and another 1024 // 8. `forget_bias`: every entry is at least 3 and at most ln(1024) + 1.7.
All inputs are finite; a program needn't handle non-finite values.
Results may differ from a plain program's by a relative error of at most 0.02.
Values may be sent and summed in bfloat16 or wider, within the bound.
A program may use at most 128 MiB of HBM per device.

v0:
```python
import jax
import jax.numpy as jnp
from jax import lax
from jax.sharding import PartitionSpec as P

BLOCK = 64


epsilon = 1e-05


def add_columns(operand, weights_piece):
    return jnp.dot(operand, weights_piece, preferred_element_type=jnp.float32)


def project_output(source_rows, weights):
    return jnp.dot(
        source_rows,
        lax.all_gather(weights, "req", axis=1, tiled=True),
        preferred_element_type=jnp.float32,
    )


def block_step(carried, forget_block, value_block, query_block, start_row, lengths):
    steps_here = forget_block.shape[1]
    positions = start_row + jnp.arange(steps_here, dtype=jnp.int32)
    alive_mask = (positions[None, :] < lengths[:, None])[:, :, None, None]
    log_forget = jnp.where(alive_mask, jax.nn.log_sigmoid(forget_block), 0.0)
    key_gate = jnp.where(alive_mask, jax.nn.sigmoid(-forget_block), 0.0)
    cumulated = jnp.cumsum(log_forget, axis=1)
    query_tilde = query_block * jnp.exp(cumulated)
    key_tilde = key_gate * jnp.exp(-cumulated)
    scores = jnp.einsum("pthc,pshc->phts", query_tilde, key_tilde, precision=lax.Precision.HIGHEST)
    triangle = jnp.arange(steps_here)[:, None] >= jnp.arange(steps_here)[None, :]
    scores = jnp.where(triangle, scores, 0.0)
    emitted = jnp.einsum("phts,pshv->pthv", scores, value_block, precision=lax.Precision.HIGHEST)
    emitted = emitted + jnp.einsum(
        "pthc,phcv->pthv", query_tilde, carried, precision=lax.Precision.HIGHEST
    )
    emitted = jnp.where(alive_mask, emitted, 0.0)
    last_log = cumulated[:, -1]
    key_decayed = key_gate * jnp.exp(last_log[:, None] - cumulated)
    carried = jnp.exp(last_log)[..., None] * carried + jnp.einsum(
        "pthc,pthv->phcv", key_decayed, value_block, precision=lax.Precision.HIGHEST
    )
    return (carried, emitted)


def on_device(
    prompt_tokens,
    decode_tokens,
    prompt_lengths,
    decode_states,
    w_fio,
    forget_bias,
    head_gain,
    w_out,
    mlp_gain,
    w_gu,
    w_down,
):
    prompts_here, plen, feature_part = prompt_tokens.shape
    heads_here = decode_states.shape[1]
    head_size = decode_states.shape[2]
    prompt_rows = prompts_here * plen
    local_rows = jnp.concatenate(
        [prompt_tokens.reshape(prompt_rows, feature_part), decode_tokens], axis=0
    )
    row_count = local_rows.shape[0]
    x_full = lax.all_gather(local_rows, "mlp", axis=1, tiled=True)
    model_width = x_full.shape[1]
    mixing = add_columns(
        x_full, lax.all_gather(w_fio.astype(jnp.bfloat16), "req", axis=0, tiled=True)
    )
    mixing = mixing.reshape(row_count, heads_here, 3, head_size)
    bias_table = forget_bias.reshape(heads_here, head_size)
    forget_logit = mixing[:, :, 0] + bias_table
    values = mixing[:, :, 1]
    queries = mixing[:, :, 2]
    prompt_forget = forget_logit[:prompt_rows].reshape(prompts_here, plen, heads_here, head_size)
    prompt_values = values[:prompt_rows].reshape(prompts_here, plen, heads_here, head_size)
    prompt_queries = queries[:prompt_rows].reshape(prompts_here, plen, heads_here, head_size)
    start_state = jnp.zeros((prompts_here, heads_here, head_size, head_size), jnp.float32)
    block_total = plen // BLOCK

    def to_blocks(source_array):
        return source_array.reshape(
            prompts_here, block_total, BLOCK, heads_here, head_size
        ).transpose(1, 0, 2, 3, 4)

    def scan_block(carried, inputs):
        forget_block, value_block, query_block, start_row = inputs
        return block_step(
            carried, forget_block, value_block, query_block, start_row, prompt_lengths
        )

    starts = jnp.arange(block_total, dtype=jnp.int32) * BLOCK
    prompt_states, block_outputs = lax.scan(
        scan_block,
        start_state,
        (to_blocks(prompt_forget), to_blocks(prompt_values), to_blocks(prompt_queries), starts),
    )
    prompt_mixed = block_outputs.transpose(1, 0, 2, 3, 4).reshape(
        prompts_here, plen, heads_here, head_size
    )
    decode_logit = forget_logit[prompt_rows:]
    decode_next = (
        jax.nn.sigmoid(decode_logit)[..., None] * decode_states
        + jax.nn.sigmoid(-decode_logit)[..., None] * values[prompt_rows:][:, :, None, :]
    )
    decode_mixed = jnp.einsum(
        "nhcv,nhc->nhv", decode_next, queries[prompt_rows:], precision=lax.Precision.HIGHEST
    )
    mixed_all = jnp.concatenate(
        [prompt_mixed.reshape(prompt_rows, heads_here, head_size), decode_mixed], axis=0
    )
    mean_square = jnp.mean(mixed_all * mixed_all, axis=-1, keepdims=True)
    head_rows = (
        mixed_all * lax.rsqrt(mean_square + epsilon) * head_gain.reshape(heads_here, head_size)
    ).astype(jnp.bfloat16)
    head_rows = head_rows.reshape(row_count, heads_here * head_size)
    offset = lax.axis_index("mlp") * feature_part
    head_terms = project_output(head_rows, w_out.astype(jnp.bfloat16))
    attention = lax.psum_scatter(
        head_terms.astype(jnp.bfloat16), "mlp", scatter_dimension=1, tiled=True
    ).astype(jnp.float32)
    residual = (local_rows.astype(jnp.float32) + attention).astype(jnp.bfloat16)
    residual_wide = residual.astype(jnp.float32)
    square_sum = lax.psum(jnp.sum(residual_wide * residual_wide, axis=1), "mlp")
    row_scale = lax.rsqrt(square_sum / model_width + epsilon)[:, None]
    gain_part = lax.dynamic_slice_in_dim(mlp_gain, offset, feature_part)
    normed_part = (residual_wide * row_scale * gain_part).astype(jnp.bfloat16)
    normed = lax.all_gather(normed_part, "mlp", axis=1, tiled=True)
    gate_up = add_columns(
        normed, lax.all_gather(w_gu.astype(jnp.bfloat16), "req", axis=0, tiled=True)
    )
    hidden_here = w_gu.shape[1] // 2
    hidden = (jax.nn.silu(gate_up[:, :hidden_here]) * gate_up[:, hidden_here:]).astype(jnp.bfloat16)
    down_terms = jnp.dot(
        hidden,
        lax.all_gather(w_down.astype(jnp.bfloat16), "req", axis=1, tiled=True),
        preferred_element_type=jnp.float32,
    )
    down_share = lax.psum_scatter(
        down_terms.astype(jnp.bfloat16), "mlp", scatter_dimension=1, tiled=True
    ).astype(jnp.float32)
    layer_output = (residual_wide + down_share).astype(jnp.bfloat16)
    prompt_out = layer_output[:prompt_rows].reshape(prompts_here, plen, feature_part)
    decode_out = layer_output[prompt_rows:]
    return (prompt_out, decode_out, prompt_states, decode_next)


def solution(mesh):
    placed = (
        P("req", None, "mlp"),
        P("req", "mlp"),
        P("req"),
        P("req", "mlp", None, None),
        P("req", "mlp"),
        P("mlp"),
        P("mlp"),
        P("mlp", "req"),
        P(),
        P("req", "mlp"),
        P("mlp", "req"),
    )
    return jax.shard_map(
        on_device,
        mesh=mesh,
        in_specs=placed,
        out_specs=(
            P("req", None, "mlp"),
            P("req", "mlp"),
            P("req", "mlp", None, None),
            P("req", "mlp", None, None),
        ),
        check_vma=False,
    )
```

profile of v0, /device:TPU:0, one launch (start us, length us, event | category | flops | bytes accessed | tf_op | source)
XLA Modules:
  0.0 746.3 jit_solution(9309867673790380533)
XLA Ops:
  7.2 2.4 convert_element_type.47
  12.2 44.9 %all-gather.9.cloned.1.call-done = bf16[2048,768]{1,0:T(8,128)(2,1)} async-done(((bf16[512,768]{1,0:T(8,128)(2,1)}), bf16[2048,768]{1,0:T(8,128)(2,1)}) %all-gather.9.cloned.1.call-update) | async-done | bytes 3145744 | tf_op jit(solution)/shard_map/all_gather | solution.py:73
  57.1 84.4 %all-gather.7.cloned.1.call-done = bf16[2052,2048]{1,0:T(8,128)(2,1)} async-done(((bf16[2052,256]{1,0:T(8,128)(2,1)}), bf16[2052,2048]{1,0:T(8,128)(2,1)}) %all-gather.7.cloned.1.call-update) | async-done | bytes 8405008 | tf_op jit(solution)/shard_map/all_gather | solution.py:70
  141.5 11.2 %fusion.48 = f32[2052,768]{0,1:T(8,128)S(1)} fusion(bf16[2052,2048]{1,0:T(8,128)(2,1)} %all-gather.7.cloned.1.call-done, bf16[2048,768]{1,0:T(8,128)(2,1)} %all-gather.9.cloned.1.call-done), kind=kOutput, calls=%fused_computation.85 | convolution fusion | flops 6455033856 | bytes 17854464 | tf_op jit(solution)/shard_map/dot_general | solution.py:13
  152.9 2.6 copy-done.5
  155.5 2.5 fusion.47
  161.8 3.7 copy.60
  165.5 3.1 copy.61
  168.5 157.8 %while.13 = (s32[]{:T(128)}, f32[2,2,128,128]{3,2,1,0:T(8,128)}, f32[16,2,64,2,128]{4,2,3,1,0:T(8,128)}, s32[16]{0:T(128)}, s32[2]{0:T(128)S(1)}, /*index=5*/f32...) while((s32[]{:T(128)}, f32[2,2,128,128]{3,2,1,0:T(8,128)}, ...), condition=%wide.region_2.3_spmd.clone, body=%wide.region_0.2_spmd.clone.sunk | while | flops 154063040 | bytes 4221876 | solution.py:98
  175.1 2.3 convolution_add_fusion.2
  184.9 2.4 convolution_add_fusion.2
  191.5 2.0 fusion.79
  194.8 2.4 convolution_add_fusion.2
  201.4 2.0 fusion.79
  204.8 2.4 convolution_add_fusion.2
  211.3 2.0 fusion.79
  214.7 2.4 convolution_add_fusion.2
  221.3 2.0 fusion.79
  224.6 2.4 convolution_add_fusion.2
  231.2 2.0 fusion.79
  234.5 2.4 convolution_add_fusion.2
  241.1 2.0 fusion.79
  244.5 2.4 convolution_add_fusion.2
  251.1 2.0 fusion.79
  254.4 2.4 convolution_add_fusion.2
  261.0 2.0 fusion.79
  264.3 2.4 convolution_add_fusion.2
  270.9 2.0 fusion.79
  274.3 2.4 convolution_add_fusion.2
  280.9 2.0 fusion.79
  284.2 2.4 convolution_add_fusion.2
  294.1 2.4 convolution_add_fusion.2
  300.7 2.0 fusion.79
  304.1 2.4 convolution_add_fusion.2
  314.0 2.4 convolution_add_fusion.2
  320.6 2.0 fusion.79
  323.9 2.4 convolution_add_fusion.2
  331.9 4.7 mul.103
  342.4 7.5 %convolution_convert_fusion.1 = bf16[2052,2048]{1,0:T(8,128)(2,1)} fusion(bf16[256,2048]{1,0:T(8,128)(2,1)} %all-gather.11.cloned.1.call-done, f32[2052,256]{1,0:T(8,128)S(1)} %bitcast.130, f32[4,256]{1,0:T(4,128)S(1)} %bitcast.144, f32[2048,256]{1,0:T(8,128)} %bitcast.136, f32[256]{0:T(256)S(1)} %copy-done.11), kind=kOutput, calls=%fused_computation.51 | convolution fusion | flops 2157981696 | bytes 13657088 | tf_op jit(solution)/shard_map/dot_general | solution.py:17
  350.0 3.1 convert_element_type.55
  354.0 84.5 %reduce-scatter.3.cloned.1.call-done = bf16[2052,256]{1,0:T(8,128)(2,1)} async-done(((bf16[2052,2048]{1,0:T(8,128)(2,1)}), bf16[2052,256]{1,0:T(8,128)(2,1)}) %reduce-scatter.3.cloned.1.call-update) | async-done | bytes 1050640 | tf_op jit(solution)/shard_map/reduce_scatter | solution.py:124
  440.2 25.9 %psum.7 = f32[2052]{0:T(1024)S(1)} all-reduce(f32[2052]{0:T(1024)S(1)} %fusion.36), channel_id=1, replica_groups=mesh['req'=4,'mlp'=8] {'mlp'}, use_global_device_ids=true, to_apply=%region_6.7 | all-reduce | flops 2052 | bytes 16416 | tf_op jit(solution)/shard_map/psum | solution.py:129
  468.6 35.7 %all-gather.15.cloned.1.call-done = bf16[2048,1408]{1,0:T(8,128)(2,1)} async-done(((bf16[512,1408]{1,0:T(8,128)(2,1)}), bf16[2048,1408]{1,0:T(8,128)(2,1)}) %all-gather.15.cloned.1.call-update) | async-done | bytes 5767184 | tf_op jit(solution)/shard_map/all_gather | solution.py:135
  504.3 84.3 %all-gather.13.cloned.1.call-done = bf16[2052,2048]{1,0:T(8,128)(2,1)} async-done(((bf16[2052,256]{1,0:T(8,128)(2,1)}), bf16[2052,2048]{1,0:T(8,128)(2,1)}) %all-gather.13.cloned.1.call-update) | async-done | bytes 8405008 | tf_op jit(solution)/shard_map/all_gather | solution.py:133
  588.6 19.0 %fusion.50 = f32[2052,1408]{1,0:T(8,128)} fusion(bf16[2052,2048]{1,0:T(8,128)(2,1)} %all-gather.13.cloned.1.call-done, bf16[2048,1408]{1,0:T(8,128)(2,1)} %all-gather.15.cloned.1.call-done), kind=kOutput, calls=%fused_computation.87 | convolution fusion | flops 11834228736 | bytes 25729024 | tf_op jit(solution)/shard_map/dot_general | solution.py:13
  607.6 23.3 %all-gather.17.cloned.1.call-done = bf16[704,2048]{1,0:T(8,128)(2,1)} async-done(((bf16[704,512]{1,0:T(8,128)(2,1)}), bf16[704,2048]{1,0:T(8,128)(2,1)}) %all-gather.17.cloned.1.call-update) | async-done | bytes 2883600 | tf_op jit(solution)/shard_map/all_gather | solution.py:141
  630.9 15.0 %convolution_convert_fusion = bf16[2052,2048]{1,0:T(8,128)(2,1)} fusion(bf16[704,2048]{1,0:T(8,128)(2,1)} %all-gather.17.cloned.1.call-done, f32[2052,1408]{1,0:T(8,128)} %fusion.50), kind=kOutput, calls=%fused_computation.50 | convolution fusion | flops 5929984512 | bytes 23920640 | tf_op jit(solution)/shard_map/dot_general | solution.py:139
  645.9 90.3 %reduce-scatter.5.cloned.1.call-done = bf16[2052,256]{1,0:T(8,128)(2,1)} async-done(((bf16[2052,2048]{1,0:T(8,128)(2,1)}), bf16[2052,256]{1,0:T(8,128)(2,1)}) %reduce-scatter.5.cloned.1.call-update) | async-done | bytes 1050640 | tf_op jit(solution)/shard_map/reduce_scatter | solution.py:144
  (289 shorter events, 120.4 us)
Async XLA Ops:
  7.2 2.6 copy-start
  7.2 2.6 copy-start.10
  7.2 50.0 %all-gather.9.cloned.1.call-start = ((), (), s32[]{:S(2)}) async-start(), calls=%async_computation.3 | async-start | bytes 3932160 | tf_op jit(solution)/shard_map/all_gather | solution.py:73
  9.7 1.2 copy-start.9
  9.7 131.8 %all-gather.7.cloned.1.call-start = ((), (), s32[]{:S(2)}) async-start(), calls=%async_computation.2 | async-start | bytes 9474048 | tf_op jit(solution)/shard_map/all_gather | solution.py:70
  10.8 331.6 %all-gather.11.cloned.1.call-start = ((), (), s32[]{:S(2)}) async-start(), calls=%async_computation.4 | async-start | bytes 1310720 | tf_op jit(solution)/shard_map/all_gather | solution.py:19
  11.7 426.8 %reduce-scatter.3.cloned.1.call-start = ((), (), s32[]{:S(2)}) async-start(), calls=%async_computation.5 | async-start | bytes 9474048 | tf_op jit(solution)/shard_map/reduce_scatter | solution.py:124
  152.7 2.8 copy-start.5
  158.1 1.9 copy-start.12
  161.8 3.7 copy-start.2
  165.5 3.1 copy-start.13
  165.5 3.1 slice-start
  171.8 0.7 copy-start.6
  180.6 0.7 copy-start.6
  190.5 0.7 copy-start.6
  200.5 0.7 copy-start.6
  210.4 0.7 copy-start.6
  220.3 0.7 copy-start.6
  230.3 0.7 copy-start.6
  240.2 0.7 copy-start.6
  250.1 0.7 copy-start.6
  260.1 0.7 copy-start.6
  270.0 0.7 copy-start.6
  279.9 0.7 copy-start.6
  289.9 0.7 copy-start.6
  299.8 0.7 copy-start.6
  309.7 0.7 copy-start.6
  319.6 0.7 copy-start.6
  326.3 4.2 copy-start.3
  329.8 0.8 copy-start.7
  337.6 1.6 copy-start.4
  340.9 1.5 copy-start.11
  349.9 154.4 %all-gather.15.cloned.1.call-start = ((), (), s32[]{:S(2)}) async-start(), calls=%async_computation.7 | async-start | bytes 7208960 | tf_op jit(solution)/shard_map/all_gather | solution.py:135
  353.1 235.4 %all-gather.13.cloned.1.call-start = ((), (), s32[]{:S(2)}) async-start(), calls=%async_computation.6 | async-start | bytes 9474048 | tf_op jit(solution)/shard_map/all_gather | solution.py:133
  438.4 27.7 %copy-start.1 = (bf16[2052,256]{1,0:T(8,128)(2,1)S(1)}, bf16[2052,256]{1,0:T(8,128)(2,1)}, u32[]{:S(2)}) copy-start(bf16[2052,256]{1,0:T(8,128)(2,1)} %reduce-scatter.3.cloned.1.call-done) | copy-start | bytes 3151876
  466.1 1.5 copy-start.8
  467.5 163.3 %all-gather.17.cloned.1.call-start = ((), (), s32[]{:S(2)}) async-start(), calls=%async_computation.8 | async-start | bytes 3604480 | tf_op jit(solution)/shard_map/all_gather | solution.py:141
  468.6 267.7 %reduce-scatter.5.cloned.1.call-start = ((), (), s32[]{:S(2)}) async-start(), calls=%async_computation.9 | async-start | bytes 9474048 | tf_op jit(solution)/shard_map/reduce_scatter | solution.py:144
Sparse Core Ops, SparseCore 0:
  10.4 46.6 all-gather.8
  58.7 82.7 all-gather.6
  143.4 24.6 all-gather.10
  350.1 88.3 reduce-scatter.2
  440.1 64.1 all-gather.14
  505.8 82.7 all-gather.12
  591.0 39.8 all-gather.16
  646.0 90.1 reduce-scatter.4
where the time goes:
time: 749 us; the launch traced here: 746 us
  waiting for transfers between devices  447 us (60%)
  matrix products  133 us (18%)
  local copies, waits for them, and re-layouts  88.7 us (12%)
  other arithmetic  35.2 us (5%)
  blocking collectives  25.9 us (3%)
  between operations  14.4 us (2%)
    reduce_scatter x1, waiting for transfers between devices, on_device(): lax.psum_scatter(down_terms.astype(jnp.bfloat16), 'mlp', scatter_dimensio...  90.3 us
    reduce_scatter x1, waiting for transfers between devices, on_device(): lax.psum_scatter(head_terms.astype(jnp.bfloat16), 'mlp', scatter_dimensio...  84.5 us
    all_gather x1, waiting for transfers between devices, on_device(): x_full = lax.all_gather(local_rows, 'mlp', axis=1, tiled=True)  84.4 us
    all_gather x1, waiting for transfers between devices, on_device(): normed = lax.all_gather(normed_part, 'mlp', axis=1, tiled=True)  84.3 us
    all_gather x1, waiting for transfers between devices, on_device(): lax.all_gather(w_fio.astype(jnp.bfloat16), 'req', axis=0, tiled=True)  44.9 us
    dot_general x16, matrix products, block_step(): jnp.einsum('pthc,pthv->phcv', key_decayed, value_block, precision=lax.Pre...  38.7 us
    all_gather x1, waiting for transfers between devices, on_device(): lax.all_gather(w_gu.astype(jnp.bfloat16), 'req', axis=0, tiled=True)  35.7 us
    dynamic_slice x32, local copies, waits for them, and re-layouts, on_device(): lax.scan(scan_block, start_state, (to_blocks(prompt_forget), to_blocks(pr...  34.5 us
  transfers between devices with their start and end apart: 8, of which 7 were waited for; matrix products, arithmetic and copies ran while one was open for 30% of the time, Pallas kernels for 0%

commit v1 on v0

v1 whole, which is shorter than its diff:
```python
import functools

import jax
import jax.numpy as jnp
import numpy as np
from jax import lax
from jax.experimental import pallas as pl
from jax.experimental.pallas import tpu as pltpu
from jax.sharding import PartitionSpec as P

MESH = pl.DeviceIdType.MESH
EPS = 1e-05
SUB = 128
LEVELS = 7
CHUNK = 256
DEC = 16
BF = jnp.bfloat16
F32 = jnp.float32


def decay_sums():
    t = np.arange(SUB)[:, None]
    s = np.arange(SUB)[None, :]
    parts = [s <= t, s > t]
    for level in range(1, LEVELS + 1):
        block = 1 << level
        middle = (t // block) * block + block // 2 - 1
        parts.append(((s > middle) & (s <= t)) | ((s > t) & (s <= middle)))
    stacked = np.concatenate(parts, axis=0).astype(np.float32)
    return np.concatenate([stacked, stacked], axis=1)


def dot(a, b, dims=((1,), (0,))):
    return lax.dot_general(a, b, (dims, ((), ())), preferred_element_type=F32)


class Exchange:
    def __init__(self, x_ref, d_ref, full, dfull, sib_out, sib_in, z_out, z_in, keep,
                 dsib_out, dsib_in, dz_out, dz_in, dkeep, sems, extra_peers=False):
        self.req = lax.axis_index("req")
        self.me = lax.axis_index("mlp")
        self.n_req = lax.axis_size("req")
        self.chips = lax.axis_size("mlp") // 2
        self.chip = self.me // 2
        self.core = self.me % 2
        self.x, self.d = x_ref, d_ref
        self.full, self.dfull = full, dfull
        self.bufs = (sib_out, sib_in, z_out, z_in, keep)
        self.dbufs = (dsib_out, dsib_in, dz_out, dz_in, dkeep)
        (self.ga_s, self.ga_r, self.gr_s, self.sb_s, self.sb_r, self.z_s, self.z_r) = sems
        self.extra = extra_peers
        self.count = x_ref.shape[0] // CHUNK

    def sibling(self):
        return (self.req, self.chip * 2 + 1 - self.core)

    def far(self, o):
        j = lax.rem(self.chip + o, self.chips)
        return j, (self.req, j * 2 + self.core)

    def enter(self):
        barrier = pltpu.get_barrier_semaphore()
        peers = [self.sibling()] + [self.far(o)[1] for o in range(1, self.chips)]
        if self.extra:
            peers += [(lax.rem(self.req + o, self.n_req), self.me) for o in range(1, self.n_req)]
        for peer in peers:
            pl.semaphore_signal(barrier, inc=1, device_id=peer, device_id_type=MESH)
        pl.semaphore_wait(barrier, len(peers))

    def rows(self, k):
        return pl.ds(pl.multiple_of(k * CHUNK, CHUNK), CHUNK)

    def own(self, k, dec):
        return self.d if dec else self.x.at[self.rows(k)]

    def slot(self, k, src, dec):
        return self.dfull.at[src] if dec else self.full.at[src, self.rows(k)]

    def remote(self, src, dst, ssem, rsem, dev):
        return pltpu.make_async_remote_copy(
            src_ref=src, dst_ref=dst, send_sem=ssem, recv_sem=rsem, device_id=dev, device_id_type=MESH)

    def gather_copy(self, k, o, dec):
        dev = self.sibling() if o == 0 else self.far(o)[1]
        return self.remote(self.own(k, dec), self.slot(k, self.me, dec),
                           self.ga_s.at[k, o], self.ga_r.at[k, self.me], dev)

    def relay_copy(self, k, o, dec):
        src = self.far(o)[0] * 2 + self.core
        return self.remote(self.slot(k, src, dec), self.slot(k, src, dec),
                           self.gr_s.at[k, o], self.ga_r.at[k, src], self.sibling())

    def arrive(self, k, src, dec):
        slot = self.slot(k, src, dec)
        self.remote(slot, slot, self.gr_s.at[k, 0], self.ga_r.at[k, src], self.sibling()).wait_recv()

    def gather_start(self, k, dec=False):
        for o in range(1, self.chips):
            self.gather_copy(k, o, dec).start()
        self.gather_copy(k, 0, dec).start()
        if dec:
            self.dfull[self.me] = self.d[...]
        else:
            self.full[self.me, self.rows(k), :] = self.x[self.rows(k), :]

    def relay(self, k, dec=False):
        for o in range(1, self.chips):
            self.arrive(k, self.far(o)[0] * 2 + self.core, dec)
            self.relay_copy(k, o, dec).start()

    def gather_done(self, k, dec=False):
        for j in range(self.chips):
            self.arrive(k, j * 2 + 1 - self.core, dec)

    def sib_copy(self, k, dec):
        b = self.dbufs if dec else self.bufs
        src, dst = (b[0], b[1]) if dec else (b[0].at[k], b[1].at[k])
        return self.remote(src, dst, self.sb_s.at[k], self.sb_r.at[k], self.sibling())

    def share(self, k, operand, weights, dec=False):
        b = self.dbufs if dec else self.bufs
        par = lax.rem(k, 2)
        for j in range(self.chips):
            term = dot(operand, weights[j * 2 + 1 - self.core]).astype(BF)
            if dec:
                b[0][j] = term
            else:
                b[0][k, j] = term
        self.sib_copy(k, dec).start()
        for j in range(self.chips):
            term = dot(operand, weights[j * 2 + self.core])
            if dec:
                b[4][j] = term
            else:
                b[4][par, j] = term

    def z_copy(self, k, o, dec):
        b = self.dbufs if dec else self.bufs
        j, dev = self.far(o)
        src = b[2].at[j] if dec else b[2].at[k, j]
        dst = b[3].at[self.chip] if dec else b[3].at[k, self.chip]
        return self.remote(src, dst, self.z_s.at[k, o], self.z_r.at[k, self.chip], dev)

    def z_wait(self, k, o, dec):
        b = self.dbufs if dec else self.bufs
        j, dev = self.far(o)
        ref = b[3].at[j] if dec else b[3].at[k, j]
        self.remote(ref, ref, self.z_s.at[k, o], self.z_r.at[k, j], dev).wait_recv()

    def pair_sum(self, k, dec=False):
        b = self.dbufs if dec else self.bufs
        par = lax.rem(k, 2)
        self.sib_copy(k, dec).wait_recv()
        for o in list(range(1, self.chips)) + [0]:
            j = lax.rem(self.chip + o, self.chips)
            if dec:
                b[2][j] = (b[4][j] + b[1][j].astype(F32)).astype(BF)
            else:
                b[2][k, j] = (b[4][par, j] + b[1][k, j].astype(F32)).astype(BF)
            if o:
                self.z_copy(k, o, dec).start()

    def total(self, k, dec=False):
        b = self.dbufs if dec else self.bufs
        x = (self.d[...] if dec else self.x[self.rows(k), :]).astype(F32)
        acc = (b[2][self.chip] if dec else b[2][k, self.chip]).astype(F32)
        for o in range(1, self.chips):
            self.z_wait(k, o, dec)
            j = self.far(o)[0]
            acc = acc + (b[3][j] if dec else b[3][k, j]).astype(F32)
        return (x + acc).astype(BF)

    def finish(self, k, dec=False):
        for o in range(self.chips):
            self.gather_copy(k, o, dec).wait_send()
        for o in range(1, self.chips):
            self.relay_copy(k, o, dec).wait_send()
            self.z_copy(k, o, dec).wait_send()
        self.sib_copy(k, dec).wait_send()

    def run(self, work, out_ref, dout_ref, before=None):
        count = self.count
        self.enter()
        if before is not None:
            before()
        lax.fori_loop(0, count, lambda k, c: (self.gather_start(k), c)[1], 0)
        self.gather_start(count, True)
        self.relay(0)

        def body(k, c):
            @pl.when(k + 1 < count)
            def _():
                self.relay(k + 1)
            self.gather_done(k)
            work(k, False)

            @pl.when(k > 0)
            def _():
                self.pair_sum(k - 1)
            return c

        lax.fori_loop(0, count, body, 0)
        self.relay(count, True)
        self.gather_done(count, True)
        self.pair_sum(count - 1)
        work(count, True)
        self.pair_sum(count, True)

        def last(k, c):
            out_ref[self.rows(k), :] = self.total(k)
            self.finish(k)
            return c

        lax.fori_loop(0, count, last, 0)
        dout_ref[...] = self.total(count, True)
        self.finish(count, True)


def gates(z):
    u = jnp.exp(-jnp.abs(z))
    big = 1.0 / (1.0 + u)
    small = u * big
    logf = jnp.minimum(z, 0.0) - jnp.log1p(u)
    return logf, jnp.where(z >= 0, small, big), jnp.where(z >= 0, big, small)


def head_norm(o, gain):
    return (o * lax.rsqrt(jnp.mean(o * o, axis=-1, keepdims=True) + EPS) * gain).astype(BF)


def mix_kernel(heads, plen, lengths, x_ref, d_ref, wf_ref, wo_ref, bias_ref, gain_ref, sums_ref, dst_ref,
               out_ref, dout_ref, states_ref, next_ref,
               wf, wo, state, ws_s, ws_r, full, dfull, *rest):
    ex = Exchange(x_ref, d_ref, full, dfull, *rest[:10], rest[10:], extra_peers=True)
    n_mlp, feat = full.shape[0], full.shape[2]
    per = wf_ref.shape[0] // feat
    dk = dst_ref.shape[-1]
    decodes = dst_ref.shape[0]
    req = ex.req

    def w_copy(i, o, mine):
        peer = lax.rem(req + o, ex.n_req)
        owner = req if mine else peer
        ref = wo.at[pl.ds(owner * per, per)] if i else wf.at[owner]
        return ex.remote(ref, ref, ws_s.at[i, o], ws_r.at[i, owner], (peer, ex.me))

    def before():
        wf[req] = wf_ref[...].astype(BF)
        for p in range(per):
            wo[req * per + p] = wo_ref[:, p * feat:(p + 1) * feat].astype(BF)
        for i in range(2):
            for o in range(1, ex.n_req):
                w_copy(i, o, True).start()

    def mixing(block):
        acc = None
        for s in range(n_mlp):
            term = dot(block(s), wf[s // per, (s % per) * feat:(s % per + 1) * feat, :])
            acc = term if acc is None else acc + term
        return acc

    def step(m, k, sub):
        p = (k * CHUNK) // plen
        row0 = lax.rem(k * CHUNK, plen) + sub * SUB
        row = row0 + lax.broadcasted_iota(jnp.int32, (SUB, dk), 0)
        alive = row < lengths[p]
        lg, kg = [], []
        for h in range(heads):
            z = m[:, h * 3 * dk:h * 3 * dk + dk] + bias_ref[:, h * dk:(h + 1) * dk]
            logf, key, _ = gates(z)
            lg.append(jnp.where(alive, logf, 0.0))
            kg.append(jnp.where(alive, key, 0.0))
        lf = jnp.concatenate(lg, axis=1) if heads > 1 else lg[0]
        hi = lf.astype(BF)
        lo = (lf - hi.astype(F32)).astype(BF)
        decays = jnp.exp(dot(sums_ref[...], jnp.concatenate([hi, lo], axis=0)))
        t = lax.broadcasted_iota(jnp.int32, (SUB, SUB), 0)
        s = lax.broadcasted_iota(jnp.int32, (SUB, SUB), 1)
        outs = []
        for h in range(heads):
            cols = slice(h * dk, (h + 1) * dk)
            v = m[:, h * 3 * dk + dk:h * 3 * dk + 2 * dk]
            q = m[:, h * 3 * dk + 2 * dk:h * 3 * dk + 3 * dk]
            k_ = kg[h]
            v16 = v.astype(BF)
            head = decays[0:SUB, cols]
            tail = decays[SUB:2 * SUB, cols]
            old = jnp.where(row0 == 0, 0.0, state[h])
            o = dot((q * head).astype(BF), old.astype(BF), ((1,), (1,)))
            scores = None
            for level in range(LEVELS, 0, -1):
                e = decays[(level + 1) * SUB:(level + 2) * SUB, cols]
                right = (lax.broadcasted_iota(jnp.int32, (SUB, dk), 0) >> (level - 1)) & 1
                qt = jnp.where(right == 1, q * e, 0.0).astype(BF)
                kt = jnp.where(right == 1, 0.0, k_ * e).astype(BF)
                term = dot(qt, kt, ((1,), (1,)))
                if level == LEVELS:
                    scores = term
                else:
                    scores = scores + jnp.where((t >> level) == (s >> level), term, 0.0)
            o = o + dot(scores.astype(BF), v16)
            o = o + jnp.sum(q * k_, axis=-1, keepdims=True) * v
            outs.append(jnp.where(alive, o, 0.0))
            new = old * head[SUB - 1:SUB, :] + dot(v16, (k_ * tail).astype(BF), ((0,), (0,)))
            state[h] = new
            states_ref[p, h] = new.T
        return outs

    def normed(outs):
        rows = [head_norm(o, gain_ref[:, h * dk:(h + 1) * dk]) for h, o in enumerate(outs)]
        return jnp.concatenate(rows, axis=1) if heads > 1 else rows[0]

    def decode(m):
        outs = []
        pad = jnp.zeros((dk - DEC, dk), F32)
        for h in range(heads):
            z = m[:, h * 3 * dk:h * 3 * dk + dk] + bias_ref[:, h * dk:(h + 1) * dk]
            _, key, f = gates(z)
            v = m[:, h * 3 * dk + dk:h * 3 * dk + 2 * dk]
            q = m[:, h * 3 * dk + 2 * dk:h * 3 * dk + 3 * dk]
            f_t = jnp.concatenate([f, pad], axis=0).T
            k_t = jnp.concatenate([key, pad], axis=0).T
            q_t = jnp.concatenate([q, pad], axis=0).T
            rows = []
            for n in range(decodes):
                new = f_t[:, n:n + 1] * dst_ref[n, h] + k_t[:, n:n + 1] * v[n:n + 1, :]
                next_ref[n, h] = new
                rows.append(jnp.sum(q_t[:, n:n + 1] * new, axis=0, keepdims=True))
            rows.append(jnp.zeros((DEC - decodes, dk), F32))
            outs.append(jnp.concatenate(rows, axis=0))
        return normed(outs)

    def work(k, dec):
        if dec:
            m = mixing(lambda s: dfull[s])
            ex.share(k, decode(m), wo, True)
            return

        @pl.when(k == 0)
        def _():
            for o in range(1, ex.n_req):
                for i in range(2):
                    w_copy(i, o, False).wait_recv()
        m = mixing(lambda s: full[s, ex.rows(k), :])
        pieces = [normed(step(m[i * SUB:(i + 1) * SUB], k, i)) for i in range(CHUNK // SUB)]
        ex.share(k, jnp.concatenate(pieces, axis=0), wo)

    ex.run(work, out_ref, dout_ref, before)
    for o in range(1, ex.n_req):
        for i in range(2):
            w_copy(i, o, True).wait_send()


def mlp_kernel(x_ref, d_ref, gain_ref, wgu, wd, out_ref, dout_ref, full, dfull, *rest):
    ex = Exchange(x_ref, d_ref, full, dfull, *rest[:10], rest[10:])
    n_mlp, feat = full.shape[0], full.shape[2]
    per = wgu.shape[2] // feat
    width = n_mlp * feat

    def work(k, dec):
        def block(s):
            return (dfull[s] if dec else full[s, ex.rows(k), :]).astype(F32)
        total = None
        for s in range(n_mlp):
            x = block(s)
            part = jnp.sum(x * x, axis=-1, keepdims=True)
            total = part if total is None else total + part
        scale = lax.rsqrt(total / width + EPS)
        gate = up = None
        for s in range(n_mlp):
            x = (block(s) * scale * gain_ref[:, s * feat:(s + 1) * feat]).astype(BF)
            part = slice((s % per) * feat, (s % per + 1) * feat)
            g = dot(x, wgu[s // per, 0, part, :])
            u = dot(x, wgu[s // per, 1, part, :])
            gate = g if gate is None else gate + g
            up = u if up is None else up + u
        hidden = (gate / (1.0 + jnp.exp(-gate)) * up).astype(BF)
        ex.share(k, hidden, wd, dec)

    ex.run(work, out_ref, dout_ref)


def exchange_scratch(n_mlp, count, feat):
    chips = n_mlp // 2
    dma = pltpu.SemaphoreType.DMA
    big = pltpu.VMEM((count, chips, CHUNK, feat), BF)
    small = pltpu.VMEM((chips, DEC, feat), BF)
    return [
        pltpu.VMEM((n_mlp, count * CHUNK, feat), BF),
        pltpu.VMEM((n_mlp, DEC, feat), BF),
        big, big, big, big, pltpu.VMEM((2, chips, CHUNK, feat), F32),
        small, small, small, small, pltpu.VMEM((chips, DEC, feat), F32),
        dma((count + 1, chips)), dma((count + 1, n_mlp)), dma((count + 1, chips)),
        dma((count + 1,)), dma((count + 1,)), dma((count + 1, chips)), dma((count + 1, chips)),
    ]


def on_device(n_req, n_mlp, prompt_tokens, decode_tokens, prompt_lengths, decode_states, w_fio, forget_bias,
              head_gain, w_out, mlp_gain, w_gu, w_down):
    prompts, plen, feat = prompt_tokens.shape
    decodes, heads, dk, _ = decode_states.shape
    rows = prompts * plen
    count = rows // CHUNK
    per = w_fio.shape[0] // feat
    vmem = pl.BlockSpec(memory_space=pltpu.VMEM)
    x = prompt_tokens.reshape(rows, feat)
    d = jnp.pad(decode_tokens, ((0, DEC - decodes), (0, 0)))
    params = functools.partial(pltpu.CompilerParams, has_side_effects=True, vmem_limit_bytes=58 * 2**20)
    hidden = w_down.shape[0]

    gu = w_gu.astype(BF).reshape(w_gu.shape[0], 2, hidden).transpose(1, 0, 2)
    gu = lax.all_gather(gu, "req", axis=0)
    down = w_down.astype(BF).reshape(hidden, per, feat).transpose(1, 0, 2)
    down = lax.all_gather(down, "req", axis=0, tiled=True)

    dma = pltpu.SemaphoreType.DMA
    residual, dresidual, states, after = pl.pallas_call(
        functools.partial(mix_kernel, heads, plen),
        out_shape=(
            jax.ShapeDtypeStruct((rows, feat), BF),
            jax.ShapeDtypeStruct((DEC, feat), BF),
            jax.ShapeDtypeStruct((prompts, heads, dk, dk), F32),
            jax.ShapeDtypeStruct((decodes, heads, dk, dk), F32),
        ),
        in_specs=[pl.BlockSpec(memory_space=pltpu.SMEM)] + [vmem] * 8,
        out_specs=(vmem,) * 4,
        scratch_shapes=[
            pltpu.VMEM((n_req,) + w_fio.shape, BF),
            pltpu.VMEM((n_mlp, heads * dk, feat), BF),
            pltpu.VMEM((heads, dk, dk), F32),
            dma((2, n_req)), dma((2, n_req)),
        ] + exchange_scratch(n_mlp, count, feat),
        compiler_params=params(collective_id=0),
        name="mix",
    )(prompt_lengths, x, d, w_fio, w_out, forget_bias.reshape(1, -1), head_gain.reshape(1, -1),
      jnp.asarray(decay_sums(), BF), decode_states)

    out, dout = pl.pallas_call(
        mlp_kernel,
        out_shape=(jax.ShapeDtypeStruct((rows, feat), BF), jax.ShapeDtypeStruct((DEC, feat), BF)),
        in_specs=[vmem] * 5,
        out_specs=(vmem,) * 2,
        scratch_shapes=exchange_scratch(n_mlp, count, feat),
        compiler_params=params(collective_id=1),
        name="mlp",
    )(residual, dresidual, mlp_gain.reshape(1, -1), gu, down)
    return out.reshape(prompts, plen, feat), dout[:decodes], states, after


def solution(mesh):
    placed = (
        P("req", None, "mlp"),
        P("req", "mlp"),
        P("req"),
        P("req", "mlp", None, None),
        P("req", "mlp"),
        P("mlp"),
        P("mlp"),
        P("mlp", "req"),
        P(),
        P("req", "mlp"),
        P("mlp", "req"),
    )
    return jax.shard_map(
        functools.partial(on_device, mesh.shape["req"], mesh.shape["mlp"]),
        mesh=mesh,
        in_specs=placed,
        out_specs=(
            P("req", None, "mlp"),
            P("req", "mlp"),
            P("req", "mlp", None, None),
            P("req", "mlp", None, None),
        ),
        check_vma=False,
    )
```

time: 749 us -> 417 us (0.56)
  waiting for transfers between devices: 447 us -> 0.06 us
  Pallas kernels: 0 us -> 384 us
  matrix products: 133 us -> 0 us
  local copies, waits for them, and re-layouts: 88.7 us -> 18.3 us
  other arithmetic: 35.2 us -> 0.09 us
  blocking collectives: 25.9 us -> 0 us
    pallas_call x0 -> x2, Pallas kernels: none -> 384 us  [the longest x1 194 us: on_device(): pl.pallas_call(functools.partial(mix_kernel, heads, plen), out_shape=(jax...]
    all_gather x6 -> x2, waiting for transfers between devices: 273 us -> 0.02 us  [the longest x1 0.02 us: on_device(): gu = lax.all_gather(gu, 'req', axis=0)]
    reduce_scatter x2 -> x0, waiting for transfers between devices: 175 us -> none  [the longest x1 90.3 us: on_device(): lax.psum_scatter(down_terms.astype(jnp.bfloat16), 'mlp', scatter_dimensio...]
    dot_general x69 -> x0, matrix products: 133 us -> none  [the longest x16 38.7 us: block_step(): jnp.einsum('pthc,pthv->phcv', key_decayed, value_block, precision=lax.Pre...]
    dynamic_slice x33 -> x0, local copies, waits for them, and re-layouts: 35.3 us -> none  [the longest x32 34.5 us: on_device(): lax.scan(scan_block, start_state, (to_blocks(prompt_forget), to_blocks(pr...]
    psum x1 -> x0, blocking collectives: 25.9 us -> none  [on_device(): square_sum = lax.psum(jnp.sum(residual_wide * residual_wide, axis=1), 'mlp')]
    add x18 -> x0, other arithmetic: 13.6 us -> none  [the longest x16 10.3 us: block_step(): positions = start_row + jnp.arange(steps_here, dtype=jnp.int32)]
    squeeze x16 -> x0, local copies, waits for them, and re-layouts: 11 us -> none  [block_step(): last_log = cumulated[:, -1]]
  transfers between devices with their start and end apart: 8 -> 2, of which waited for: 7 -> 0; matrix products, arithmetic and copies ran while one was open for 30% -> 2% of each run, Pallas kernels for 0% -> 47%
where the time goes in v1:
time: 417 us
  Pallas kernels  384 us (92%)
  local copies, waits for them, and re-layouts  18.3 us (4%)
  between operations  14.1 us (3%)
    pallas_call x1, Pallas kernels, on_device(): pl.pallas_call(functools.partial(mix_kernel, heads, plen), out_shape=(jax...  194 us
    pallas_call x1, Pallas kernels, on_device(): pl.pallas_call(mlp_kernel, out_shape=(jax.ShapeDtypeStruct((rows, feat),...  190 us
    all_gather x1, local copies, waits for them, and re-layouts, on_device(): gu = lax.all_gather(gu, 'req', axis=0)  8.41 us
  transfers between devices with their start and end apart: 2, of which 0 were waited for; matrix products, arithmetic and copies ran while one was open for 2% of the time, Pallas kernels for 47%

profile of v1, /device:TPU:0, one launch (start us, length us, event | category | flops | bytes accessed | tf_op | source)
XLA Modules:
  0.0 417.1 jit_solution(5026426289217867157)
XLA Ops:
  7.2 0.0 copy-start
  7.2 0.0 all-gather.6.cloned.1.call-start
  7.2 3.1 copy.20
  10.3 0.0 all-gather.6.cloned.1.call-update
  10.3 0.0 copy-start.3
  10.3 0.0 all-gather.4.cloned.1.call-start
  10.4 0.0 copy-done
  10.4 0.1 convert_element_type.9
  10.5 0.2 reshape.34
  10.6 1.0 copy.22
  11.6 0.0 all-gather.4.cloned.1.call-update
  11.6 0.0 copy-done.3
  11.6 0.6 pad.4.d_ref
  12.2 194.0 %mix.1 = (bf16[2048,256]{1,0:T(8,128)(2,1)}, bf16[16,256]{1,0:T(8,128)(2,1)}, f32[2,2,128,128]{3,2,1,0:T(8,128)}, f32[4,2,128,128]{3,2,1,0:T(8,128)}) custom-call(s32[2]{0:T(128)} %lengths.1, bf16[2048,256]{1,0:T(8,128)(2,1)} %bitcast.14, bf16[16,256]{1,0:T(8,128)(2,1)} %pad.4.d_ref, f32[512,768]{1,0:T(8,128)} %wf_ref.1, f32[256,512]{1,0:T(8,128)} %wo_ref.1, ...), custom_call_target="tpu_custom_call" | custom-call | tf_op jit(solution)/shard_map/mix/pallas_call | solution.py:417
  206.2 0.0 all-gather.6.cloned.1.call-done
  206.3 8.4 %copy.21 = bf16[8,512,704]{2,1,0:T(8,128)(2,1)} copy(bf16[8,512,704]{1,2,0:T(8,128)(2,1)} %all-gather.6.cloned.1.call-done) | data formatting | bytes 11534336 | tf_op jit(solution)/shard_map/all_gather | solution.py:412
  214.7 0.0 all-gather.4.cloned.1.call-done.wd
  214.7 0.0 copy-start.2
  214.7 190.4 %mlp.1 = (bf16[2048,256]{1,0:T(8,128)(2,1)}, bf16[16,256]{1,0:T(8,128)(2,1)}) custom-call(bf16[2048,256]{1,0:T(8,128)(2,1)} %get-tuple-element.10.x_ref, bf16[16,256]{1,0:T(8,128)(2,1)} %get-tuple-element.11.d_ref, f32[1,2048]{1,0:T(1,128)} %bitcast.15, bf16[4,2,512,704]{3,2,1,0:T(8,128)(2,1)} %bitcast.10, bf16[8,704,256]{2,1,0:T(8,128)(2,1)} %all-gather.4.cloned.1.call-done.wd), custom_call_target="tpu_custom_call" | custom-call | tf_op jit(solution)/shard_map/mlp/pallas_call | solution.py:438
  405.1 0.0 copy-start.1
  405.1 1.3 slice.3
  406.5 2.3 copy.26
  408.7 0.0 copy-done.2
  408.7 0.7 copy.27
  409.4 0.0 copy-done.1
  409.4 0.8 copy.28
Async XLA Ops:
  7.2 3.2 copy-start
  7.2 199.1 %all-gather.6.cloned.1.call-start = ((), (), s32[]{:S(2)}) async-start(), calls=%async_computation.1 | async-start | bytes 7208960 | tf_op jit(solution)/shard_map/all_gather | solution.py:412
  10.3 1.3 copy-start.3
  10.3 204.4 %all-gather.4.cloned.1.call-start = ((), (), s32[]{:S(2)}) async-start(), calls=%async_computation | async-start | bytes 3604480 | tf_op jit(solution)/shard_map/all_gather | solution.py:414
  214.7 194.0 %copy-start.2 = (f32[2,2,128,128]{3,2,1,0:T(8,128)S(1)}, f32[2,2,128,128]{3,2,1,0:T(8,128)}, u32[]{:S(2)}) copy-start(f32[2,2,128,128]{3,2,1,0:T(8,128)} %get-tuple-element.22) | copy-start | bytes 786436
  405.1 4.3 %copy-start.1 = (f32[4,2,128,128]{3,2,1,0:T(8,128)S(1)}, f32[4,2,128,128]{3,2,1,0:T(8,128)}, u32[]{:S(2)}) copy-start(f32[4,2,128,128]{3,2,1,0:T(8,128)} %get-tuple-element.23) | copy-start | bytes 1572868
Sparse Core Ops, SparseCore 0:
  10.4 102.7 all-gather.5
  115.7 40.8 all-gather.3

commit v2 on v1

--- a/solution.py
+++ b/solution.py
@@ -35,8 +35,7 @@
 
 
 class Exchange:
-    def __init__(self, x_ref, d_ref, full, dfull, sib_out, sib_in, z_out, z_in, keep,
-                 dsib_out, dsib_in, dz_out, dz_in, dkeep, sems, extra_peers=False):
+    def __init__(self, x_ref, d_ref, full, dfull, bufs, dbufs, tot, sems, extra_peers=False):
         self.req = lax.axis_index("req")
         self.me = lax.axis_index("mlp")
         self.n_req = lax.axis_size("req")
@@ -45,9 +44,11 @@
         self.core = self.me % 2
         self.x, self.d = x_ref, d_ref
         self.full, self.dfull = full, dfull
-        self.bufs = (sib_out, sib_in, z_out, z_in, keep)
-        self.dbufs = (dsib_out, dsib_in, dz_out, dz_in, dkeep)
-        (self.ga_s, self.ga_r, self.gr_s, self.sb_s, self.sb_r, self.z_s, self.z_r) = sems
+        self.sib_out, self.sib_in, self.sums, self.z_in, self.keep = bufs
+        self.dbufs = dbufs
+        self.tot = tot
+        (self.line_s, self.pair_s, self.got, self.dga_s, self.dgr_s, self.dgot,
+         self.sb_s, self.sb_r, self.z_s, self.z_r, self.dz_s, self.dz_r) = sems
         self.extra = extra_peers
         self.count = x_ref.shape[0] // CHUNK
 
@@ -57,6 +58,10 @@
     def far(self, o):
         j = lax.rem(self.chip + o, self.chips)
         return j, (self.req, j * 2 + self.core)
+
+    def beside(self, right):
+        j = self.chip + (1 if right else -1)
+        return (self.req, j * 2 + self.core)
 
     def enter(self):
         barrier = pltpu.get_barrier_semaphore()
@@ -70,150 +75,219 @@
     def rows(self, k):
         return pl.ds(pl.multiple_of(k * CHUNK, CHUNK), CHUNK)
 
-    def own(self, k, dec):
-        return self.d if dec else self.x.at[self.rows(k)]
-
-    def slot(self, k, src, dec):
-        return self.dfull.at[src] if dec else self.full.at[src, self.rows(k)]
-
     def remote(self, src, dst, ssem, rsem, dev):
         return pltpu.make_async_remote_copy(
             src_ref=src, dst_ref=dst, send_sem=ssem, recv_sem=rsem, device_id=dev, device_id_type=MESH)
 
-    def gather_copy(self, k, o, dec):
+
+    def has(self, right):
+        return self.chip + 1 < self.chips if right else self.chip > 0
+
+    def block_copy(self, k, h, from_left, to):
+        src_chip = self.chip - h if from_left else self.chip + h
+        source = src_chip * 2 + self.core
+        slot = self.full.at[source, self.rows(k)]
+        src = slot if h else self.x.at[self.rows(k)]
+        if to == "line":
+            sem = self.line_s.at[k, self.chips if h == 0 and not from_left else src_chip]
+            dev = self.beside(from_left)
+        else:
+            sem, dev = self.pair_s.at[k, src_chip], self.sibling()
+        return self.remote(src, slot, sem, self.got.at[k, source], dev)
+
+    def each_send(self, k, h, act):
+        for from_left in (True, False):
+            there = self.chip - h >= 0 if from_left else self.chip + h < self.chips
+
+            def go(from_left=from_left):
+                if h and act == "start":
+                    source = (self.chip - h if from_left else self.chip + h) * 2 + self.core
+                    slot = self.full.at[source, self.rows(k)]
+                    self.remote(slot, slot, self.pair_s.at[k, 0], self.got.at[k, source], self.sibling()).wait_recv()
+
+                @pl.when(self.has(from_left))
+                def _():
+                    copy = self.block_copy(k, h, from_left, "line")
+                    copy.start() if act == "start" else copy.wait_send()
+                if h or from_left:
+                    copy = self.block_copy(k, h, from_left, "pair")
+                    copy.start() if act == "start" else copy.wait_send()
+            if h:
+                pl.when(there)(go)
+            else:
+                go()
+
+    def hop(self, k, h):
+        self.each_send(k, h, "start")
+        if h == 0:
+            self.full[self.me, self.rows(k), :] = self.x[self.rows(k), :]
+
+    def gather_done(self, k):
+        for j in range(self.chips):
+            source = j * 2 + 1 - self.core
+            slot = self.full.at[source, self.rows(k)]
+            self.remote(slot, slot, self.pair_s.at[k, 0], self.got.at[k, source], self.sibling()).wait_recv()
+
+
+    def dgather_copy(self, o):
         dev = self.sibling() if o == 0 else self.far(o)[1]
-        return self.remote(self.own(k, dec), self.slot(k, self.me, dec),
-                           self.ga_s.at[k, o], self.ga_r.at[k, self.me], dev)
-
-    def relay_copy(self, k, o, dec):
+        return self.remote(self.d, self.dfull.at[self.me], self.dga_s.at[o], self.dgot.at[self.me], dev)
+
+    def drelay_copy(self, o):
         src = self.far(o)[0] * 2 + self.core
-        return self.remote(self.slot(k, src, dec), self.slot(k, src, dec),
-                           self.gr_s.at[k, o], self.ga_r.at[k, src], self.sibling())
-
-    def arrive(self, k, src, dec):
-        slot = self.slot(k, src, dec)
-        self.remote(slot, slot, self.gr_s.at[k, 0], self.ga_r.at[k, src], self.sibling()).wait_recv()
-
-    def gather_start(self, k, dec=False):
+        return self.remote(self.dfull.at[src], self.dfull.at[src], self.dgr_s.at[o], self.dgot.at[src], self.sibling())
+
+    def darrive(self, src):
+        slot = self.dfull.at[src]
+        self.remote(slot, slot, self.dgr_s.at[0], self.dgot.at[src], self.sibling()).wait_recv()
+
+    def dgather_start(self):
+        for o in range(self.chips):
+            self.dgather_copy(o).start()
+        self.dfull[self.me] = self.d[...]
+
+    def drelay(self):
         for o in range(1, self.chips):
-            self.gather_copy(k, o, dec).start()
-        self.gather_copy(k, 0, dec).start()
-        if dec:
-            self.dfull[self.me] = self.d[...]
-        else:
-            self.full[self.me, self.rows(k), :] = self.x[self.rows(k), :]
-
-    def relay(self, k, dec=False):
-        for o in range(1, self.chips):
-            self.arrive(k, self.far(o)[0] * 2 + self.core, dec)
-            self.relay_copy(k, o, dec).start()
-
-    def gather_done(self, k, dec=False):
-        for j in range(self.chips):
-            self.arrive(k, j * 2 + 1 - self.core, dec)
+            self.darrive(self.far(o)[0] * 2 + self.core)
+            self.drelay_copy(o).start()
+
+    def dgather_done(self):
+        for j in range(self.chips):
+            self.darrive(j * 2 + 1 - self.core)
+
 
     def sib_copy(self, k, dec):
-        b = self.dbufs if dec else self.bufs
-        src, dst = (b[0], b[1]) if dec else (b[0].at[k], b[1].at[k])
+        src, dst = self.dbufs[:2] if dec else (self.sib_out.at[k], self.sib_in.at[k])
         return self.remote(src, dst, self.sb_s.at[k], self.sb_r.at[k], self.sibling())
 
     def share(self, k, operand, weights, dec=False):
-        b = self.dbufs if dec else self.bufs
         par = lax.rem(k, 2)
         for j in range(self.chips):
             term = dot(operand, weights[j * 2 + 1 - self.core]).astype(BF)
             if dec:
-                b[0][j] = term
+                self.dbufs[0][j] = term
             else:
-                b[0][k, j] = term
+                self.sib_out[k, j] = term
         self.sib_copy(k, dec).start()
         for j in range(self.chips):
             term = dot(operand, weights[j * 2 + self.core])
             if dec:
-                b[4][j] = term
+                self.dbufs[4][j] = term
             else:
-                b[4][par, j] = term
-
-    def z_copy(self, k, o, dec):
-        b = self.dbufs if dec else self.bufs
+                self.keep[par, j] = term
+
+    def pair_sum(self, k):
+        par = lax.rem(k, 2)
+        self.sib_copy(k, False).wait_recv()
+        for j in range(self.chips):
+            self.sums[k, j] = (self.keep[par, j] + self.sib_in[k, j].astype(F32)).astype(BF)
+
+    def sum_copy(self, k, j, right):
+        place = j if right else jnp.where(self.chip - 1 == j, self.chips, j)
+        return self.remote(self.sums.at[k, j], self.z_in.at[k, place], self.z_s.at[k, j], self.z_r.at[k, place],
+                           self.beside(right))
+
+    def sum_wait(self, k, place):
+        ref = self.z_in.at[k, place]
+        self.remote(ref, ref, self.z_s.at[k, 0], self.z_r.at[k, place], self.sibling()).wait_recv()
+
+    def chain(self, k, right):
+        for j in range(self.chips):
+            @pl.when(self.chip < j if right else self.chip > j)
+            def _():
+                @pl.when(self.has(not right))
+                def _():
+                    self.sum_wait(k, j)
+                    self.sums[k, j] = (self.sums[k, j].astype(F32) + self.z_in[k, j].astype(F32)).astype(BF)
+                self.sum_copy(k, j, right).start()
+
+    def total(self, k, out_ref):
+        self.tot[...] = self.x[self.rows(k), :].astype(F32) + self.sums[k, self.chip].astype(F32)
+        for right, place in ((False, self.chip), (True, self.chips)):
+            @pl.when(self.has(right))
+            def _():
+                self.sum_wait(k, place)
+                self.tot[...] += self.z_in[k, place].astype(F32)
+        out_ref[self.rows(k), :] = self.tot[...].astype(BF)
+
+    def dz_copy(self, o):
         j, dev = self.far(o)
-        src = b[2].at[j] if dec else b[2].at[k, j]
-        dst = b[3].at[self.chip] if dec else b[3].at[k, self.chip]
-        return self.remote(src, dst, self.z_s.at[k, o], self.z_r.at[k, self.chip], dev)
-
-    def z_wait(self, k, o, dec):
-        b = self.dbufs if dec else self.bufs
-        j, dev = self.far(o)
-        ref = b[3].at[j] if dec else b[3].at[k, j]
-        self.remote(ref, ref, self.z_s.at[k, o], self.z_r.at[k, j], dev).wait_recv()
-
-    def pair_sum(self, k, dec=False):
-        b = self.dbufs if dec else self.bufs
-        par = lax.rem(k, 2)
-        self.sib_copy(k, dec).wait_recv()
+        return self.remote(self.dbufs[2].at[j], self.dbufs[3].at[self.chip], self.dz_s.at[o],
+                           self.dz_r.at[self.chip], dev)
+
+    def dpair_sum(self):
+        b = self.dbufs
+        self.sib_copy(self.count, True).wait_recv()
         for o in list(range(1, self.chips)) + [0]:
-            j = lax.rem(self.chip + o, self.chips)
-            if dec:
-                b[2][j] = (b[4][j] + b[1][j].astype(F32)).astype(BF)
-            else:
-                b[2][k, j] = (b[4][par, j] + b[1][k, j].astype(F32)).astype(BF)
+            j = self.far(o)[0]
+            b[2][j] = (b[4][j] + b[1][j].astype(F32)).astype(BF)
             if o:
-                self.z_copy(k, o, dec).start()
-
-    def total(self, k, dec=False):
-        b = self.dbufs if dec else self.bufs
-        x = (self.d[...] if dec else self.x[self.rows(k), :]).astype(F32)
-        acc = (b[2][self.chip] if dec else b[2][k, self.chip]).astype(F32)
+                self.dz_copy(o).start()
+
+    def dtotal(self, out_ref):
+        b = self.dbufs
+        acc = self.d[...].astype(F32) + b[2][self.chip].astype(F32)
         for o in range(1, self.chips):
-            self.z_wait(k, o, dec)
-            j = self.far(o)[0]
-            acc = acc + (b[3][j] if dec else b[3][k, j]).astype(F32)
-        return (x + acc).astype(BF)
-
-    def finish(self, k, dec=False):
+            j, dev = self.far(o)
+            ref = b[3].at[j]
+            self.remote(ref, ref, self.dz_s.at[o], self.dz_r.at[j], dev).wait_recv()
+            acc = acc + b[3][j].astype(F32)
+        out_ref[...] = acc.astype(BF)
         for o in range(self.chips):
-            self.gather_copy(k, o, dec).wait_send()
+            self.dgather_copy(o).wait_send()
         for o in range(1, self.chips):
-            self.relay_copy(k, o, dec).wait_send()
-            self.z_copy(k, o, dec).wait_send()
-        self.sib_copy(k, dec).wait_send()
+            self.drelay_copy(o).wait_send()
+            self.dz_copy(o).wait_send()
+        self.sib_copy(self.count, True).wait_send()
+
+    def finish(self, k):
+        for h in range(self.chips):
+            self.each_send(k, h, "wait")
+        self.sib_copy(k, False).wait_send()
+        for j in range(self.chips):
+            for right in (True, False):
+                @pl.when(self.chip < j if right else self.chip > j)
+                def _():
+                    self.sum_copy(k, j, right).wait_send()
 
     def run(self, work, out_ref, dout_ref, before=None):
-        count = self.count
+        count, chips = self.count, self.chips
+
+        def at(k, action):
+            @pl.when((k >= 0) & (k < count))
+            def _():
+                action(k)
+
         self.enter()
         if before is not None:
             before()
-        lax.fori_loop(0, count, lambda k, c: (self.gather_start(k), c)[1], 0)
-        self.gather_start(count, True)
-        self.relay(0)
-
-        def body(k, c):
-            @pl.when(k + 1 < count)
+        self.dgather_start()
+
+        def body(step, c):
+            i = step - chips
+            for h in range(chips):
+                at(i + chips - h, functools.partial(self.hop, h=h))
+            pl.when(i == 1)(self.drelay)
+
+            def compute(k):
+                self.gather_done(k)
+                work(k, False)
+            at(i, compute)
+
+            @pl.when(i == 2)
             def _():
-                self.relay(k + 1)
-            self.gather_done(k)
-            work(k, False)
-
-            @pl.when(k > 0)
-            def _():
-                self.pair_sum(k - 1)
+                self.dgather_done()
+                work(count, True)
+            pl.when(i == 3)(self.dpair_sum)
+            at(i - 1, self.pair_sum)
+            at(i - 1 - self.chip, functools.partial(self.chain, right=True))
+            at(i - chips + self.chip, functools.partial(self.chain, right=False))
+            at(i - chips - 1, functools.partial(self.total, out_ref=out_ref))
             return c
 
-        lax.fori_loop(0, count, body, 0)
-        self.relay(count, True)
-        self.gather_done(count, True)
-        self.pair_sum(count - 1)
-        work(count, True)
-        self.pair_sum(count, True)
-
-        def last(k, c):
-            out_ref[self.rows(k), :] = self.total(k)
-            self.finish(k)
-            return c
-
-        lax.fori_loop(0, count, last, 0)
-        dout_ref[...] = self.total(count, True)
-        self.finish(count, True)
+        lax.fori_loop(0, count + 2 * chips + 1, body, 0)
+        self.dtotal(dout_ref)
+        lax.fori_loop(0, count, lambda k, c: (self.finish(k), c)[1], 0)
 
 
 def gates(z):
@@ -228,10 +302,10 @@
     return (o * lax.rsqrt(jnp.mean(o * o, axis=-1, keepdims=True) + EPS) * gain).astype(BF)
 
 
-def mix_kernel(heads, plen, lengths, x_ref, d_ref, wf_ref, wo_ref, bias_ref, gain_ref, sums_ref, dst_ref,
-               out_ref, dout_ref, states_ref, next_ref,
-               wf, wo, state, ws_s, ws_r, full, dfull, *rest):
-    ex = Exchange(x_ref, d_ref, full, dfull, *rest[:10], rest[10:], extra_peers=True)
+def mix_kernel(heads, plen, lengths, x_ref, d_ref, wf_ref, wo_ref, bias_ref, gain_ref, sums_ref, dst_ref, gu_ref, down_ref,
+               out_ref, dout_ref, states_ref, next_ref, gu_out, down_out,
+               wf, wo, state, ws_s, ws_r, own_s, full, dfull, *rest):
+    ex = Exchange(x_ref, d_ref, full, dfull, rest[:5], rest[5:10], rest[10], rest[11:], extra_peers=True)
     n_mlp, feat = full.shape[0], full.shape[2]
     per = wf_ref.shape[0] // feat
     dk = dst_ref.shape[-1]
@@ -241,8 +315,19 @@
     def w_copy(i, o, mine):
         peer = lax.rem(req + o, ex.n_req)
         owner = req if mine else peer
-        ref = wo.at[pl.ds(owner * per, per)] if i else wf.at[owner]
-        return ex.remote(ref, ref, ws_s.at[i, o], ws_r.at[i, owner], (peer, ex.me))
+        if i == 0:
+            src = dst = wf.at[owner]
+        elif i == 1:
+            src = dst = wo.at[pl.ds(owner * per, per)]
+        elif i == 2:
+            src, dst = gu_ref, gu_out.at[owner]
+        else:
+            src, dst = down_ref, down_out.at[pl.ds(owner * per, per)]
+        return ex.remote(src, dst, ws_s.at[i, o], ws_r.at[i, owner], (peer, ex.me))
+
+    def own_copies():
+        return (pltpu.make_async_copy(gu_ref, gu_out.at[req], own_s.at[0]),
+                pltpu.make_async_copy(down_ref, down_out.at[pl.ds(req * per, per)], own_s.at[1]))
 
     def before():
         wf[req] = wf_ref[...].astype(BF)
@@ -341,18 +426,27 @@
             for o in range(1, ex.n_req):
                 for i in range(2):
                     w_copy(i, o, False).wait_recv()
+            for i in range(2, 4):
+                for o in range(1, ex.n_req):
+                    w_copy(i, o, True).start()
+            for copy in own_copies():
+                copy.start()
         m = mixing(lambda s: full[s, ex.rows(k), :])
         pieces = [normed(step(m[i * SUB:(i + 1) * SUB], k, i)) for i in range(CHUNK // SUB)]
         ex.share(k, jnp.concatenate(pieces, axis=0), wo)
 
     ex.run(work, out_ref, dout_ref, before)
     for o in range(1, ex.n_req):
-        for i in range(2):
+        for i in range(4):
             w_copy(i, o, True).wait_send()
+        for i in range(2, 4):
+            w_copy(i, o, False).wait_recv()
+    for copy in own_copies():
+        copy.wait()
 
 
 def mlp_kernel(x_ref, d_ref, gain_ref, wgu, wd, out_ref, dout_ref, full, dfull, *rest):
-    ex = Exchange(x_ref, d_ref, full, dfull, *rest[:10], rest[10:])
+    ex = Exchange(x_ref, d_ref, full, dfull, rest[:5], rest[5:10], rest[10], rest[11:])
     n_mlp, feat = full.shape[0], full.shape[2]
     per = wgu.shape[2] // feat
     width = n_mlp * feat
@@ -388,10 +482,13 @@
     return [
         pltpu.VMEM((n_mlp, count * CHUNK, feat), BF),
         pltpu.VMEM((n_mlp, DEC, feat), BF),
-        big, big, big, big, pltpu.VMEM((2, chips, CHUNK, feat), F32),
+        big, big, big, pltpu.VMEM((count, chips + 1, CHUNK, feat), BF), pltpu.VMEM((2, chips, CHUNK, feat), F32),
         small, small, small, small, pltpu.VMEM((chips, DEC, feat), F32),
-        dma((count + 1, chips)), dma((count + 1, n_mlp)), dma((count + 1, chips)),
-        dma((count + 1,)), dma((count + 1,)), dma((count + 1, chips)), dma((count + 1, chips)),
+        pltpu.VMEM((CHUNK, feat), F32),
+        dma((count, chips + 1)), dma((count, chips)), dma((count, n_mlp)),
+        dma((chips,)), dma((chips,)), dma((n_mlp,)),
+        dma((count + 1,)), dma((count + 1,)), dma((count, chips)), dma((count, chips + 1)),
+        dma((chips,)), dma((chips,)),
     ]
 
 
@@ -403,37 +500,38 @@
     count = rows // CHUNK
     per = w_fio.shape[0] // feat
     vmem = pl.BlockSpec(memory_space=pltpu.VMEM)
+    anywhere = pl.BlockSpec(memory_space=pl.ANY)
     x = prompt_tokens.reshape(rows, feat)
     d = jnp.pad(decode_tokens, ((0, DEC - decodes), (0, 0)))
     params = functools.partial(pltpu.CompilerParams, has_side_effects=True, vmem_limit_bytes=58 * 2**20)
     hidden = w_down.shape[0]
 
     gu = w_gu.astype(BF).reshape(w_gu.shape[0], 2, hidden).transpose(1, 0, 2)
-    gu = lax.all_gather(gu, "req", axis=0)
     down = w_down.astype(BF).reshape(hidden, per, feat).transpose(1, 0, 2)
-    down = lax.all_gather(down, "req", axis=0, tiled=True)
 
     dma = pltpu.SemaphoreType.DMA
-    residual, dresidual, states, after = pl.pallas_call(
+    residual, dresidual, states, after, gu, down = pl.pallas_call(
         functools.partial(mix_kernel, heads, plen),
         out_shape=(
             jax.ShapeDtypeStruct((rows, feat), BF),
             jax.ShapeDtypeStruct((DEC, feat), BF),
             jax.ShapeDtypeStruct((prompts, heads, dk, dk), F32),
             jax.ShapeDtypeStruct((decodes, heads, dk, dk), F32),
+            jax.ShapeDtypeStruct((n_req,) + gu.shape, BF),
+            jax.ShapeDtypeStruct((n_mlp,) + down.shape[1:], BF),
         ),
-        in_specs=[pl.BlockSpec(memory_space=pltpu.SMEM)] + [vmem] * 8,
-        out_specs=(vmem,) * 4,
+        in_specs=[pl.BlockSpec(memory_space=pltpu.SMEM)] + [vmem] * 8 + [anywhere] * 2,
+        out_specs=(vmem,) * 4 + (anywhere,) * 2,
         scratch_shapes=[
             pltpu.VMEM((n_req,) + w_fio.shape, BF),
             pltpu.VMEM((n_mlp, heads * dk, feat), BF),
             pltpu.VMEM((heads, dk, dk), F32),
-            dma((2, n_req)), dma((2, n_req)),
+            dma((4, n_req)), dma((4, n_req)), dma((2,)),
         ] + exchange_scratch(n_mlp, count, feat),
         compiler_params=params(collective_id=0),
         name="mix",
     )(prompt_lengths, x, d, w_fio, w_out, forget_bias.reshape(1, -1), head_gain.reshape(1, -1),
-      jnp.asarray(decay_sums(), BF), decode_states)
+      jnp.asarray(decay_sums(), BF), decode_states, gu, down)
 
     out, dout = pl.pallas_call(
         mlp_kernel,

time: 417 us -> 300 us (0.72)
  Pallas kernels: 384 us -> 287 us
  between operations: 14.1 us -> 0.68 us
  local copies, waits for them, and re-layouts: 18.3 us -> 10.9 us
    pallas_call x1, Pallas kernels: 190 us -> 129 us  [on_device(): pl.pallas_call(mlp_kernel, out_shape=(jax.ShapeDtypeStruct((rows, feat),...]
    pallas_call x1, Pallas kernels: 194 us -> 158 us  [on_device(): pl.pallas_call(functools.partial(mix_kernel, heads, plen), out_shape=(jax...]
    all_gather x1 -> x0, local copies, waits for them, and re-layouts: 8.41 us -> none  [on_device(): gu = lax.all_gather(gu, 'req', axis=0)]
  transfers between devices with their start and end apart: 2 -> 0, of which waited for: 0 -> 0; matrix products, arithmetic and copies ran while one was open for 2% -> 0% of each run, Pallas kernels for 47% -> 0%
where the time goes in v2:
time: 300 us
  Pallas kernels  287 us (96%)
  local copies, waits for them, and re-layouts  10.9 us (4%)
    pallas_call x1, Pallas kernels, on_device(): pl.pallas_call(functools.partial(mix_kernel, heads, plen), out_shape=(jax...  158 us
    pallas_call x1, Pallas kernels, on_device(): pl.pallas_call(mlp_kernel, out_shape=(jax.ShapeDtypeStruct((rows, feat),...  129 us

profile of v2, /device:TPU:0, one launch (start us, length us, event | category | flops | bytes accessed | tf_op | source)
XLA Modules:
  0.0 300.2 jit_solution(8570869439204290824)
XLA Ops:
  0.6 1.3 pad.4.d_ref
  1.9 1.5 convert_element_type.9
  3.4 0.9 copy.21
  4.3 2.1 copy.16
  6.4 1.6 copy.17
  7.9 158.1 %mix.1 = (bf16[2048,256]{1,0:T(8,128)(2,1)}, bf16[16,256]{1,0:T(8,128)(2,1)}, f32[2,2,128,128]{3,2,1,0:T(8,128)}, f32[4,2,128,128]{3,2,1,0:T(8,128)}, bf16[4,2,5...) custom-call(s32[2]{0:T(128)} %lengths.1, bf16[2048,256]{1,0:T(8,128)(2,1)} %bitcast.18, bf16[16,256]{1,0:T(8,128)(2,1)} %pad.4.d_ref, ...), custom_call_target="tpu_custom_call" | custom-call | tf_op jit(solution)/shard_map/mix/pallas_call | solution.py:513
  166.1 129.0 %mlp.1 = (bf16[2048,256]{1,0:T(8,128)(2,1)}, bf16[16,256]{1,0:T(8,128)(2,1)}) custom-call(bf16[2048,256]{1,0:T(8,128)(2,1)} %get-tuple-element.12.x_ref, bf16[16,256]{1,0:T(8,128)(2,1)} %get-tuple-element.13.d_ref, f32[1,2048]{1,0:T(1,128)} %bitcast.20, bf16[4,2,512,704]{3,2,1,0:T(8,128)(2,1)} %get-tuple-element.14.wgu, ...), custom_call_target="tpu_custom_call" | custom-call | tf_op jit(solution)/shard_map/mlp/pallas_call | solution.py:536
  295.1 0.0 copy-start.1
  295.1 0.0 copy-start
  295.1 1.3 slice.3
  296.5 2.3 copy.25
  298.7 0.0 copy-done.1
  298.7 0.7 copy.26
  299.4 0.0 copy-done
  299.4 0.8 copy.27
Async XLA Ops:
  295.1 3.6 %copy-start.1 = (f32[2,2,128,128]{3,2,1,0:T(8,128)S(1)}, f32[2,2,128,128]{3,2,1,0:T(8,128)}, u32[]{:S(2)}) copy-start(f32[2,2,128,128]{3,2,1,0:T(8,128)} %get-tuple-element.26) | copy-start | bytes 786436
  295.1 4.3 %copy-start = (f32[4,2,128,128]{3,2,1,0:T(8,128)S(1)}, f32[4,2,128,128]{3,2,1,0:T(8,128)}, u32[]{:S(2)}) copy-start(f32[4,2,128,128]{3,2,1,0:T(8,128)} %get-tuple-element.27) | copy-start | bytes 1572868

commit v3 on v2

--- a/solution.py
+++ b/solution.py
@@ -12,7 +12,7 @@
 EPS = 1e-05
 SUB = 128
 LEVELS = 7
-CHUNK = 256
+CHUNK = 128
 DEC = 16
 BF = jnp.bfloat16
 F32 = jnp.float32
@@ -250,7 +250,7 @@
                 def _():
                     self.sum_copy(k, j, right).wait_send()
 
-    def run(self, work, out_ref, dout_ref, before=None):
+    def run(self, work, out_ref, dout_ref, lead, before=None, hooks=()):
         count, chips = self.count, self.chips
 
         def at(k, action):
@@ -264,9 +264,11 @@
         self.dgather_start()
 
         def body(step, c):
-            i = step - chips
+            i = step - lead
             for h in range(chips):
-                at(i + chips - h, functools.partial(self.hop, h=h))
+                at(i + lead - h, functools.partial(self.hop, h=h))
+            for when, action in hooks:
+                pl.when(i == when)(action)
             pl.when(i == 1)(self.drelay)
 
             def compute(k):
@@ -285,7 +287,7 @@
             at(i - chips - 1, functools.partial(self.total, out_ref=out_ref))
             return c
 
-        lax.fori_loop(0, count + 2 * chips + 1, body, 0)
+        lax.fori_loop(0, count + lead + chips + 1, body, 0)
         self.dtotal(dout_ref)
         lax.fori_loop(0, count, lambda k, c: (self.finish(k), c)[1], 0)
 
@@ -312,18 +314,57 @@
     decodes = dst_ref.shape[0]
     req = ex.req
 
-    def w_copy(i, o, mine):
-        peer = lax.rem(req + o, ex.n_req)
-        owner = req if mine else peer
+    square = ex.n_req == 4
+    if square:
+        x_peer = req + 1 - 2 * (req % 2)
+        y_peer = lax.rem(req + 2, 4)
+        cross = lax.rem(x_peer + 2, 4)
+        ways, relays = (0, 1), (2, 3)
+        targets = (x_peer, y_peer, y_peer, x_peer)
+    else:
+        ways, relays = tuple(range(1, ex.n_req)), ()
+
+    def place(i, owner, half=None):
+        buf = (wf, wo, gu_out, down_out)[i]
+        rows = slice(None)
+        if half is not None:
+            n = buf.shape[2 if i == 2 else 1] // 2
+            rows = pl.ds(half * n, n)
         if i == 0:
-            src = dst = wf.at[owner]
-        elif i == 1:
-            src = dst = wo.at[pl.ds(owner * per, per)]
-        elif i == 2:
-            src, dst = gu_ref, gu_out.at[owner]
+            return buf.at[owner, rows]
+        if i == 2:
+            return buf.at[owner, :, rows]
+        return buf.at[pl.ds(owner * per, per), rows]
+
+    def w_send(i, way):
+        if way in relays:
+            ref = place(i, (x_peer, y_peer)[way - 2], way - 2)
+            return ex.remote(ref, ref, ws_s.at[i, way], ws_r.at[i, way], (targets[way], ex.me))
+        src = gu_ref if i == 2 else down_ref if i == 3 else place(i, req)
+        peer = targets[way] if square else lax.rem(req + way, ex.n_req)
+        at = way if square else req
+        return ex.remote(src, place(i, req), ws_s.at[i, way], ws_r.at[i, at], (peer, ex.me))
+
+    def w_wait(i, way):
+        if way in relays:
+            ref, at = place(i, cross, way - 2), way
+        elif square:
+            ref, at = place(i, targets[way]), way
         else:
-            src, dst = down_ref, down_out.at[pl.ds(owner * per, per)]
-        return ex.remote(src, dst, ws_s.at[i, o], ws_r.at[i, owner], (peer, ex.me))
+            at = lax.rem(req + way, ex.n_req)
+            ref = place(i, at)
+        peer = lax.rem(req + 1, ex.n_req)
+        ex.remote(ref, ref, ws_s.at[i, way], ws_r.at[i, at], (peer, ex.me)).wait_recv()
+
+    def w_all(items, which, act):
+        for i in items:
+            for way in which:
+                if act == "start":
+                    w_send(i, way).start()
+                elif act == "sent":
+                    w_send(i, way).wait_send()
+                else:
+                    w_wait(i, way)
 
     def own_copies():
         return (pltpu.make_async_copy(gu_ref, gu_out.at[req], own_s.at[0]),
@@ -333,9 +374,18 @@
         wf[req] = wf_ref[...].astype(BF)
         for p in range(per):
             wo[req * per + p] = wo_ref[:, p * feat:(p + 1) * feat].astype(BF)
-        for i in range(2):
-            for o in range(1, ex.n_req):
-                w_copy(i, o, True).start()
+        w_all((0, 1), ways, "start")
+
+    def first_relay():
+        w_all((0, 1), ways, "wait")
+        w_all((0, 1), relays, "start")
+        w_all((2, 3), ways, "start")
+        for copy in own_copies():
+            copy.start()
+
+    def second_relay():
+        w_all((2, 3), ways, "wait")
+        w_all((2, 3), relays, "start")
 
     def mixing(block):
         acc = None
@@ -423,24 +473,16 @@
 
         @pl.when(k == 0)
         def _():
-            for o in range(1, ex.n_req):
-                for i in range(2):
-                    w_copy(i, o, False).wait_recv()
-            for i in range(2, 4):
-                for o in range(1, ex.n_req):
-                    w_copy(i, o, True).start()
-            for copy in own_copies():
-                copy.start()
+            w_all((0, 1), relays, "wait")
         m = mixing(lambda s: full[s, ex.rows(k), :])
         pieces = [normed(step(m[i * SUB:(i + 1) * SUB], k, i)) for i in range(CHUNK // SUB)]
         ex.share(k, jnp.concatenate(pieces, axis=0), wo)
 
-    ex.run(work, out_ref, dout_ref, before)
-    for o in range(1, ex.n_req):
-        for i in range(4):
-            w_copy(i, o, True).wait_send()
-        for i in range(2, 4):
-            w_copy(i, o, False).wait_recv()
+    lead = max(ex.chips, ex.count * 3 // 4)
+    ex.run(work, out_ref, dout_ref, lead, before, ((lead // 2 - lead, first_relay), (ex.count // 2, second_relay)))
+    w_all((2, 3), relays, "wait")
+    for i in range(4):
+        w_all((i,), ways + relays, "sent")
     for copy in own_copies():
         copy.wait()
 
@@ -471,7 +513,7 @@
         hidden = (gate / (1.0 + jnp.exp(-gate)) * up).astype(BF)
         ex.share(k, hidden, wd, dec)
 
-    ex.run(work, out_ref, dout_ref)
+    ex.run(work, out_ref, dout_ref, ex.chips)
 
 
 def exchange_scratch(n_mlp, count, feat):

time: 300 us -> 289 us (0.963)
  Pallas kernels: 287 us -> 276 us
    pallas_call x1, Pallas kernels: 158 us -> 151 us  [on_device(): pl.pallas_call(functools.partial(mix_kernel, heads, plen), out_shape=(jax...]
    pallas_call x1, Pallas kernels: 129 us -> 125 us  [on_device(): pl.pallas_call(mlp_kernel, out_shape=(jax.ShapeDtypeStruct((rows, feat),...]
where the time goes in v3:
time: 289 us
  Pallas kernels  276 us (96%)
  local copies, waits for them, and re-layouts  10.9 us (4%)
    pallas_call x1, Pallas kernels, on_device(): pl.pallas_call(functools.partial(mix_kernel, heads, plen), out_shape=(jax...  151 us
    pallas_call x1, Pallas kernels, on_device(): pl.pallas_call(mlp_kernel, out_shape=(jax.ShapeDtypeStruct((rows, feat),...  125 us
    unnamed x8, local copies, waits for them, and re-layouts  5.85 us

profile of v3, /device:TPU:0, one launch (start us, length us, event | category | flops | bytes accessed | tf_op | source)
XLA Modules:
  0.0 288.9 jit_solution(6167645373298699787)
XLA Ops:
  0.6 1.3 pad.4.d_ref
  1.9 1.5 convert_element_type.9
  3.4 0.9 copy.21
  4.3 2.1 copy.16
  6.4 1.6 copy.17
  7.9 151.0 %mix.1 = (bf16[2048,256]{1,0:T(8,128)(2,1)}, bf16[16,256]{1,0:T(8,128)(2,1)}, f32[2,2,128,128]{3,2,1,0:T(8,128)}, f32[4,2,128,128]{3,2,1,0:T(8,128)}, bf16[4,2,5...) custom-call(s32[2]{0:T(128)} %lengths.1, bf16[2048,256]{1,0:T(8,128)(2,1)} %bitcast.18, bf16[16,256]{1,0:T(8,128)(2,1)} %pad.4.d_ref, ...), custom_call_target="tpu_custom_call" | custom-call | tf_op jit(solution)/shard_map/mix/pallas_call | solution.py:555
  159.0 124.8 %mlp.1 = (bf16[2048,256]{1,0:T(8,128)(2,1)}, bf16[16,256]{1,0:T(8,128)(2,1)}) custom-call(bf16[2048,256]{1,0:T(8,128)(2,1)} %get-tuple-element.12.x_ref, bf16[16,256]{1,0:T(8,128)(2,1)} %get-tuple-element.13.d_ref, f32[1,2048]{1,0:T(1,128)} %bitcast.20, bf16[4,2,512,704]{3,2,1,0:T(8,128)(2,1)} %get-tuple-element.14.wgu, ...), custom_call_target="tpu_custom_call" | custom-call | tf_op jit(solution)/shard_map/mlp/pallas_call | solution.py:578
  283.8 0.0 copy-start.1
  283.8 0.0 copy-start
  283.8 1.3 slice.3
  285.1 2.3 copy.25
  287.4 0.0 copy-done.1
  287.4 0.7 copy.26
  288.1 0.0 copy-done
  288.1 0.8 copy.27
Async XLA Ops:
  283.8 3.6 %copy-start.1 = (f32[2,2,128,128]{3,2,1,0:T(8,128)S(1)}, f32[2,2,128,128]{3,2,1,0:T(8,128)}, u32[]{:S(2)}) copy-start(f32[2,2,128,128]{3,2,1,0:T(8,128)} %get-tuple-element.26) | copy-start | bytes 786436
  283.8 4.3 %copy-start = (f32[4,2,128,128]{3,2,1,0:T(8,128)S(1)}, f32[4,2,128,128]{3,2,1,0:T(8,128)}, u32[]{:S(2)}) copy-start(f32[4,2,128,128]{3,2,1,0:T(8,128)} %get-tuple-element.27) | copy-start | bytes 1572868

commit v4 on v3

--- a/solution.py
+++ b/solution.py
@@ -12,7 +12,7 @@
 EPS = 1e-05
 SUB = 128
 LEVELS = 7
-CHUNK = 128
+CHUNK = 256
 DEC = 16
 BF = jnp.bfloat16
 F32 = jnp.float32
@@ -192,7 +192,7 @@
         self.remote(ref, ref, self.z_s.at[k, 0], self.z_r.at[k, place], self.sibling()).wait_recv()
 
     def chain(self, k, right):
-        for j in range(self.chips):
+        for j in reversed(range(self.chips)) if right else range(self.chips):
             @pl.when(self.chip < j if right else self.chip > j)
             def _():
                 @pl.when(self.has(not right))
@@ -232,7 +232,7 @@
             ref = b[3].at[j]
             self.remote(ref, ref, self.dz_s.at[o], self.dz_r.at[j], dev).wait_recv()
             acc = acc + b[3][j].astype(F32)
-        out_ref[...] = acc.astype(BF)
+        out_ref[...] = acc[:out_ref.shape[0]].astype(BF)
         for o in range(self.chips):
             self.dgather_copy(o).wait_send()
         for o in range(1, self.chips):
@@ -265,7 +265,7 @@
 
         def body(step, c):
             i = step - lead
-            for h in range(chips):
+            for h in reversed(range(chips)):
                 at(i + lead - h, functools.partial(self.hop, h=h))
             for when, action in hooks:
                 pl.when(i == when)(action)
@@ -304,10 +304,12 @@
     return (o * lax.rsqrt(jnp.mean(o * o, axis=-1, keepdims=True) + EPS) * gain).astype(BF)
 
 
-def mix_kernel(heads, plen, lengths, x_ref, d_ref, wf_ref, wo_ref, bias_ref, gain_ref, sums_ref, dst_ref, gu_ref, down_ref,
+def mix_kernel(heads, plen, lengths, x_ref, d_ref, wf_ref, wo_ref, bias_ref, gain_ref, sums_ref, dst_ref, wgu_ref, wd_ref,
                out_ref, dout_ref, states_ref, next_ref, gu_out, down_out,
-               wf, wo, state, ws_s, ws_r, own_s, full, dfull, *rest):
-    ex = Exchange(x_ref, d_ref, full, dfull, rest[:5], rest[5:10], rest[10], rest[11:], extra_peers=True)
+               wf, wo, gu_ref, down_ref, dpad, state, ws_s, ws_r, own_s, full, dfull, *rest):
+    ex = Exchange(x_ref, dpad, full, dfull, rest[:5], rest[5:10], rest[10], rest[11:], extra_peers=True)
+    spare = jnp.zeros((DEC - d_ref.shape[0], d_ref.shape[1]), F32)
+    dpad[...] = jnp.concatenate([d_ref[...].astype(F32), spare], axis=0).astype(BF)
     n_mlp, feat = full.shape[0], full.shape[2]
     per = wf_ref.shape[0] // feat
     dk = dst_ref.shape[-1]
@@ -376,9 +378,18 @@
             wo[req * per + p] = wo_ref[:, p * feat:(p + 1) * feat].astype(BF)
         w_all((0, 1), ways, "start")
 
-    def first_relay():
-        w_all((0, 1), ways, "wait")
-        w_all((0, 1), relays, "start")
+    def fio_relay():
+        w_all((0,), ways, "wait")
+        w_all((0,), relays, "start")
+
+    def out_relay():
+        hidden = wd_ref.shape[0]
+        gu_ref[0] = wgu_ref[:, :hidden].astype(BF)
+        gu_ref[1] = wgu_ref[:, hidden:].astype(BF)
+        for p in range(per):
+            down_ref[p] = wd_ref[:, p * feat:(p + 1) * feat].astype(BF)
+        w_all((1,), ways, "wait")
+        w_all((1,), relays, "start")
         w_all((2, 3), ways, "start")
         for copy in own_copies():
             copy.start()
@@ -473,13 +484,18 @@
 
         @pl.when(k == 0)
         def _():
-            w_all((0, 1), relays, "wait")
+            w_all((0,), relays, "wait")
         m = mixing(lambda s: full[s, ex.rows(k), :])
         pieces = [normed(step(m[i * SUB:(i + 1) * SUB], k, i)) for i in range(CHUNK // SUB)]
+
+        @pl.when(k == 0)
+        def _():
+            w_all((1,), relays, "wait")
         ex.share(k, jnp.concatenate(pieces, axis=0), wo)
 
     lead = max(ex.chips, ex.count * 3 // 4)
-    ex.run(work, out_ref, dout_ref, lead, before, ((lead // 2 - lead, first_relay), (ex.count // 2, second_relay)))
+    hooks = ((lead // 3 - lead, fio_relay), (lead // 2 - lead, out_relay), (ex.count // 2, second_relay))
+    ex.run(work, out_ref, dout_ref, lead, before, hooks)
     w_all((2, 3), relays, "wait")
     for i in range(4):
         w_all((i,), ways + relays, "sent")
@@ -544,12 +560,11 @@
     vmem = pl.BlockSpec(memory_space=pltpu.VMEM)
     anywhere = pl.BlockSpec(memory_space=pl.ANY)
     x = prompt_tokens.reshape(rows, feat)
-    d = jnp.pad(decode_tokens, ((0, DEC - decodes), (0, 0)))
     params = functools.partial(pltpu.CompilerParams, has_side_effects=True, vmem_limit_bytes=58 * 2**20)
     hidden = w_down.shape[0]
 
-    gu = w_gu.astype(BF).reshape(w_gu.shape[0], 2, hidden).transpose(1, 0, 2)
-    down = w_down.astype(BF).reshape(hidden, per, feat).transpose(1, 0, 2)
+    gu_block = (2, w_gu.shape[0], hidden)
+    down_block = (per, hidden, feat)
 
     dma = pltpu.SemaphoreType.DMA
     residual, dresidual, states, after, gu, down = pl.pallas_call(
@@ -559,32 +574,35 @@
             jax.ShapeDtypeStruct((DEC, feat), BF),
             jax.ShapeDtypeStruct((prompts, heads, dk, dk), F32),
             jax.ShapeDtypeStruct((decodes, heads, dk, dk), F32),
-            jax.ShapeDtypeStruct((n_req,) + gu.shape, BF),
-            jax.ShapeDtypeStruct((n_mlp,) + down.shape[1:], BF),
+            jax.ShapeDtypeStruct((n_req,) + gu_block, BF),
+            jax.ShapeDtypeStruct((n_mlp,) + down_block[1:], BF),
         ),
-        in_specs=[pl.BlockSpec(memory_space=pltpu.SMEM)] + [vmem] * 8 + [anywhere] * 2,
+        in_specs=[pl.BlockSpec(memory_space=pltpu.SMEM)] + [vmem] * 10,
         out_specs=(vmem,) * 4 + (anywhere,) * 2,
         scratch_shapes=[
             pltpu.VMEM((n_req,) + w_fio.shape, BF),
             pltpu.VMEM((n_mlp, heads * dk, feat), BF),
+            pltpu.VMEM(gu_block, BF),
+            pltpu.VMEM(down_block, BF),
+            pltpu.VMEM((DEC, feat), BF),
             pltpu.VMEM((heads, dk, dk), F32),
             dma((4, n_req)), dma((4, n_req)), dma((2,)),
         ] + exchange_scratch(n_mlp, count, feat),
         compiler_params=params(collective_id=0),
         name="mix",
-    )(prompt_lengths, x, d, w_fio, w_out, forget_bias.reshape(1, -1), head_gain.reshape(1, -1),
-      jnp.asarray(decay_sums(), BF), decode_states, gu, down)
+    )(prompt_lengths, x, decode_tokens, w_fio, w_out, forget_bias.reshape(1, -1), head_gain.reshape(1, -1),
+      jnp.asarray(decay_sums(), BF), decode_states, w_gu, w_down)
 
     out, dout = pl.pallas_call(
         mlp_kernel,
-        out_shape=(jax.ShapeDtypeStruct((rows, feat), BF), jax.ShapeDtypeStruct((DEC, feat), BF)),
+        out_shape=(jax.ShapeDtypeStruct((rows, feat), BF), jax.ShapeDtypeStruct((decodes, feat), BF)),
         in_specs=[vmem] * 5,
         out_specs=(vmem,) * 2,
         scratch_shapes=exchange_scratch(n_mlp, count, feat),
         compiler_params=params(collective_id=1),
         name="mlp",
     )(residual, dresidual, mlp_gain.reshape(1, -1), gu, down)
-    return out.reshape(prompts, plen, feat), dout[:decodes], states, after
+    return out.reshape(prompts, plen, feat), dout, states, after
 
 
 def solution(mesh):

time: 289 us -> 282 us (0.976)
  local copies, waits for them, and re-layouts: 10.9 us -> 5.07 us
where the time goes in v4:
time: 282 us
  Pallas kernels  276 us (98%)
  local copies, waits for them, and re-layouts  5.07 us (2%)
    pallas_call x1, Pallas kernels, on_device(): pl.pallas_call(functools.partial(mix_kernel, heads, plen), out_shape=(jax...  149 us
    pallas_call x1, Pallas kernels, on_device(): pl.pallas_call(mlp_kernel, out_shape=(jax.ShapeDtypeStruct((rows, feat),...  127 us

profile of v4, /device:TPU:0, one launch (start us, length us, event | category | flops | bytes accessed | tf_op | source)
XLA Modules:
  0.0 281.7 jit_solution(1168032280482284109)
XLA Ops:
  0.6 149.0 %mix.1 = (bf16[2048,256]{1,0:T(8,128)(2,1)}, bf16[16,256]{1,0:T(8,128)(2,1)}, f32[2,2,128,128]{3,2,1,0:T(8,128)}, f32[4,2,128,128]{3,2,1,0:T(8,128)}, bf16[4,2,5...) custom-call(s32[2]{0:T(128)} %lengths.1, bf16[2048,256]{1,0:T(8,128)(2,1)} %bitcast.6, bf16[4,256]{1,0:T(4,128)(2,1)} %d_ref.1, ...), custom_call_target="tpu_custom_call" | custom-call | tf_op jit(solution)/shard_map/mix/pallas_call | solution.py:570
  149.7 0.0 copy-start.1
  149.7 126.9 %mlp.1 = (bf16[2048,256]{1,0:T(8,128)(2,1)}, bf16[4,256]{1,0:T(4,128)(2,1)}) custom-call(bf16[2048,256]{1,0:T(8,128)(2,1)} %get-tuple-element.12.x_ref, bf16[16,256]{1,0:T(8,128)(2,1)} %get-tuple-element.13.d_ref, f32[1,2048]{1,0:T(1,128)} %bitcast.7, bf16[4,2,512,704]{3,2,1,0:T(8,128)(2,1)} %get-tuple-element.14.wgu, bf16[8,704,256]{2,1,0:T(8,128)(2,1)} %get-tuple-element.15.wd), custom_call_target="tpu_custom_call" | custom-call | tf_op jit(solution)/shard_map/mlp/pallas_call | solution.py:596
  276.6 0.0 copy-start
  276.6 2.3 copy.20
  278.9 1.2 copy.21
  280.2 0.0 copy-done.1
  280.2 0.7 copy.22
  280.9 0.0 copy-done
  280.9 0.8 copy.23
Async XLA Ops:
  149.7 130.5 %copy-start.1 = (f32[2,2,128,128]{3,2,1,0:T(8,128)S(1)}, f32[2,2,128,128]{3,2,1,0:T(8,128)}, u32[]{:S(2)}) copy-start(f32[2,2,128,128]{3,2,1,0:T(8,128)} %get-tuple-element.26) | copy-start | bytes 786436
  276.6 4.3 %copy-start = (f32[4,2,128,128]{3,2,1,0:T(8,128)S(1)}, f32[4,2,128,128]{3,2,1,0:T(8,128)}, u32[]{:S(2)}) copy-start(f32[4,2,128,128]{3,2,1,0:T(8,128)} %get-tuple-element.27) | copy-start | bytes 1572868
